TPU v7x, 32 devices: a whole 2x2x4 slice. The times are simulated.
32 devices in a mesh: dp: 2 (over y), context: 8 (over z, core), tensor: 2 (over x).
Axes of the slice: x: 2, y: 2, z: 4, core: 2. Of those that a mesh axis runs over, the one named last changes fastest.
Arguments:
- layer_input: bfloat16 [2, 4096, 4096], P('dp', 'context', 'tensor'), may hold values from -6 to 6
- queries: bfloat16 [2, 16, 4096, 128], P('dp', 'tensor', 'context'), may hold values from -6 to 6
- key_states: bfloat16 [2, 4, 4096, 128], P('dp', 'tensor', 'context'), may hold values from -6 to 6
- value_states: bfloat16 [2, 4, 4096, 128], P('dp', 'tensor', 'context'), may hold values from -6 to 6
- out_grad: bfloat16 [2, 16, 4096, 128], P('dp', 'tensor', 'context'), may hold values from -0.0625 to 0.0625
- log_sums: bfloat16 [2, 16, 4096], P('dp', 'tensor', 'context'), may hold values from 2 to 5
- grad_dots: bfloat16 [2, 16, 4096], P('dp', 'tensor', 'context'), may hold values from -0.5 to 0.5
- doc_stretches: int32 [2, 10], P('dp'), may hold values from 1 to 4, as said below
- stretch_order: int32 [2, 128], P('dp'), may hold values from 0 to 127, as said below
- sign_vector: int32 [32, 128], P('context'), may hold values from -1 to 1, as said below
- exponents: int32 [2, 32], P('dp', 'context'), may hold values from 0 to 3
Outputs:
- rotated_grad: float32 [32, 128, 1024], P('context', 'dp', 'tensor')
Inputs may be any that keep to these rules, and one draw needn't show every extreme that they name: `doc_stretches`: each row gives the lengths in units of 128 tokens of 10 documents; they sum to 32. The second document is one of the longest, exactly 4 units, and begins 512 - 128 tokens after a multiple of 512 tokens. `stretch_order`: each row is a permutation of the 128 sequence blocks. Sequence blocks d * 16 to d * 16 + 15 belong to index d of context; the 16 stored blocks of one index of context hold at most 2 blocks belonging to any one index. `sign_vector`: every entry is 1 or -1.
All inputs are finite; a program needn't handle non-finite values.
Results may differ from a plain program's by a relative error of at most 0.0075.
Values may be sent and summed in bfloat16 or wider, within the bound.
A program may use at most 64 MiB of HBM per device.

v0:
```python
import math

import jax
import jax.numpy as jnp
from jax import lax
from jax.sharding import PartitionSpec as P

HD = 128
GROUP = 4
BLK = 32
PAD = 128
HB = 128


def passed_along(block, axis, distance):
    devices = range(lax.axis_size(axis))
    route = [(i - distance, i) for i in devices if i - distance in devices]
    return lax.ppermute(block, axis, route)


def hadamard_table(table_size):
    index_row = jnp.arange(table_size, dtype=jnp.int32)
    common = jnp.bitwise_and(index_row[:, None], index_row[None, :])
    parity = jnp.zeros((table_size, table_size), jnp.int32)
    for bit_pos in range(table_size.bit_length() - 1):
        parity = parity + jnp.bitwise_and(jnp.right_shift(common, bit_pos), 1)
    signed = 1 - 2 * jnp.bitwise_and(parity, 1)
    return signed.astype(jnp.float32) * float(table_size) ** (-0.5)


def doc_of(position, ends_row):
    return jnp.sum(((position // PAD)[:, None] >= ends_row[None, :]).astype(jnp.int32), axis=1)


def live_pairs(query_pos, query_doc, key_pos, key_doc):
    return (query_doc[:, None] == key_doc[None, :]) & (key_pos[None, :] <= query_pos[:, None])


def block_grads(query_blk, grad_blk, lse_blk, dots_blk, key_blk, value_blk, live):
    scale = HD ** (-0.5)
    scores = (
        jnp.einsum("ghqd,gkd->ghqk", query_blk, key_blk, preferred_element_type=jnp.float32) * scale
    )
    probs = jnp.where(
        live[None, None], jnp.exp(scores - lse_blk.astype(jnp.float32)[..., None]), 0.0
    )
    value_part = jnp.einsum(
        "ghqk,ghqd->gkd", probs.astype(jnp.bfloat16), grad_blk, preferred_element_type=jnp.float32
    )
    dprobs = jnp.einsum("ghqd,gkd->ghqk", grad_blk, value_blk, preferred_element_type=jnp.float32)
    dscores = (probs * (dprobs - dots_blk.astype(jnp.float32)[..., None])).astype(jnp.bfloat16)
    key_part = (
        jnp.einsum("ghqk,ghqd->gkd", dscores, query_blk, preferred_element_type=jnp.float32) * scale
    )
    return (key_part, value_part)


def per_device(
    layer_input,
    queries,
    key_states,
    value_states,
    out_grad,
    log_sums,
    grad_dots,
    doc_stretches,
    stretch_order,
    sign_vector,
    exponents,
):
    local_tokens = queries.shape[2]
    local_kv = key_states.shape[1]
    local_cols = 2 * local_kv * HD
    order_row = stretch_order[0]
    ends_row = jnp.cumsum(doc_stretches[0])
    groups = lax.axis_size("context")
    slot_count = local_tokens // BLK
    capacity = max(1, slot_count // groups)
    device_id = lax.axis_index("context")
    order_grid = order_row.reshape(groups, slot_count)
    own_order = lax.dynamic_slice_in_dim(order_row, device_id * slot_count, slot_count, 0)
    own_target = own_order // slot_count
    slot_ids = jnp.arange(slot_count, dtype=jnp.int32)
    earlier = slot_ids[None, :] < slot_ids[:, None]
    send_rank = jnp.sum(
        jnp.where(earlier & (own_target[None, :] == own_target[:, None]), 1, 0), axis=1
    )
    send_row = own_target * capacity + send_rank
    buffer_ids = jnp.arange(groups * capacity, dtype=jnp.int32)
    send_table = (buffer_ids[:, None] == send_row[None, :]).astype(jnp.bfloat16)
    wanted = device_id * slot_count + slot_ids
    stretch_ids = jnp.arange(order_row.shape[0], dtype=jnp.int32)
    stored_at = jnp.sum(
        jnp.where(order_row[None, :] == wanted[:, None], stretch_ids[None, :], 0), axis=1
    )
    source = stored_at // slot_count
    source_slot = stored_at % slot_count
    source_orders = jnp.take(order_grid, source, axis=0)
    same_target = source_orders // slot_count == device_id
    recv_rank = jnp.sum(
        jnp.where(same_target & (slot_ids[None, :] < source_slot[:, None]), 1, 0), axis=1
    )
    recv_row = source * capacity + recv_rank
    recv_table = (recv_row[:, None] == buffer_ids[None, :]).astype(jnp.bfloat16)

    def pack(array):
        blocks = array[0].reshape(array.shape[1], slot_count, -1)
        return jnp.einsum(
            "rt,htx->rhx", send_table, blocks, preferred_element_type=jnp.float32
        ).astype(jnp.bfloat16)

    def unpack(packed):
        placed = jnp.einsum(
            "sr,rhx->hsx", recv_table, packed, preferred_element_type=jnp.float32
        ).astype(jnp.bfloat16)
        return placed.reshape(packed.shape[1], local_tokens, -1)

    moved = (
        lax.all_to_all(pack(queries), "context", split_axis=0, concat_axis=0, tiled=True),
        lax.all_to_all(pack(out_grad), "context", split_axis=0, concat_axis=0, tiled=True),
        lax.all_to_all(pack(key_states), "context", split_axis=0, concat_axis=0, tiled=True),
        lax.all_to_all(pack(value_states), "context", split_axis=0, concat_axis=0, tiled=True),
        lax.all_to_all(pack(log_sums), "context", split_axis=0, concat_axis=0, tiled=True),
        lax.all_to_all(pack(grad_dots), "context", split_axis=0, concat_axis=0, tiled=True),
    )
    query_sorted = unpack(moved[0])
    grad_sorted = unpack(moved[1])
    key_sorted = unpack(moved[2])
    value_sorted = unpack(moved[3])
    lse_sorted = unpack(moved[4])[:, :, 0]
    dots_sorted = unpack(moved[5])[:, :, 0]
    total_len = local_tokens * groups
    longest_tokens = max(total_len // PAD // 8, local_tokens // PAD) * PAD
    reach = (local_tokens - PAD + longest_tokens - 1) // local_tokens
    query_list = [query_sorted]
    grad_list = [grad_sorted]
    lse_list = [lse_sorted]
    dots_list = [dots_sorted]
    for ahead in range(1, reach + 1):
        later = passed_along(
            (query_sorted, grad_sorted, lse_sorted, dots_sorted), "context", -ahead
        )
        query_list.append(later[0])
        grad_list.append(later[1])
        lse_list.append(later[2])
        dots_list.append(later[3])
    all_query = jnp.concatenate(query_list, axis=1)
    all_grad = jnp.concatenate(grad_list, axis=1)
    all_lse = jnp.concatenate(lse_list, axis=1)
    all_dots = jnp.concatenate(dots_list, axis=1)
    total_rows = all_query.shape[1]
    query_pos_all = device_id * local_tokens + jnp.arange(total_rows, dtype=jnp.int32)
    query_doc_all = doc_of(query_pos_all, ends_row)
    key_pos_own = device_id * local_tokens + jnp.arange(local_tokens, dtype=jnp.int32)
    key_doc_own = doc_of(key_pos_own, ends_row)
    step_len = math.gcd(total_rows, 640)

    def ahead_block(index_val, running):
        offset = index_val * step_len
        query_blk = lax.dynamic_slice_in_dim(all_query, offset, step_len, 1).reshape(
            local_kv, GROUP, step_len, HD
        )
        grad_blk = lax.dynamic_slice_in_dim(all_grad, offset, step_len, 1).reshape(
            local_kv, GROUP, step_len, HD
        )
        lse_blk = lax.dynamic_slice_in_dim(all_lse, offset, step_len, 1).reshape(
            local_kv, GROUP, step_len
        )
        dots_blk = lax.dynamic_slice_in_dim(all_dots, offset, step_len, 1).reshape(
            local_kv, GROUP, step_len
        )
        query_pos = lax.dynamic_slice_in_dim(query_pos_all, offset, step_len, 0)
        query_doc = lax.dynamic_slice_in_dim(query_doc_all, offset, step_len, 0)
        live = live_pairs(query_pos, query_doc, key_pos_own, key_doc_own)
        key_part, value_part = block_grads(
            query_blk, grad_blk, lse_blk, dots_blk, key_sorted, value_sorted, live
        )
        return (running[0] + key_part, running[1] + value_part)

    empty = jnp.zeros((local_kv, local_tokens, HD), jnp.float32)
    key_total, value_total = lax.fori_loop(0, total_rows // step_len, ahead_block, (empty, empty))
    stacked = jnp.stack([key_total, value_total], axis=1)
    sorted_rows = (
        jnp.transpose(stacked, (2, 0, 1, 3))
        .reshape(slot_count, BLK * local_cols)
        .astype(jnp.bfloat16)
    )
    outgoing = jnp.einsum(
        "sr,sx->rx", recv_table, sorted_rows, preferred_element_type=jnp.float32
    ).astype(jnp.bfloat16)
    returned = lax.all_to_all(outgoing, "context", split_axis=0, concat_axis=0, tiled=True)
    stored_rows = jnp.einsum(
        "rt,rx->tx", send_table, returned, preferred_element_type=jnp.float32
    ).astype(jnp.bfloat16)
    kv_local = stored_rows.reshape(local_tokens, local_cols)[None]
    full_input = lax.all_gather(layer_input, "tensor", axis=2, tiled=True)
    row_input = lax.all_to_all(full_input, "context", split_axis=2, concat_axis=1, tiled=True)
    span = row_input[0]
    member_grad = jnp.einsum(
        "td,tc->dc",
        span,
        lax.all_gather(kv_local, "context", axis=1, tiled=True)[0],
        preferred_element_type=jnp.float32,
    )
    local_blocks = sign_vector.shape[0]
    had = hadamard_table(HB)
    shaped = (
        member_grad.reshape(local_blocks, HB, local_cols)
        * sign_vector.astype(jnp.float32)[:, :, None]
    )
    rotated = jnp.einsum("ij,bjc->bic", had, shaped, precision=lax.Precision.HIGHEST)
    factor = 1.0 / jnp.left_shift(jnp.int32(1), exponents[0]).astype(jnp.float32)
    quantized = (rotated * factor[:, None, None]).astype(jnp.bfloat16)
    spread = lax.all_to_all(quantized[None], "dp", split_axis=2, concat_axis=0, tiled=True)
    return jnp.sum(spread.astype(jnp.float32), axis=0)


def solution(mesh):
    return jax.shard_map(
        per_device,
        mesh=mesh,
        in_specs=(
            P("dp", "context", "tensor"),
            P("dp", "tensor", "context", None),
            P("dp", "tensor", "context", None),
            P("dp", "tensor", "context", None),
            P("dp", "tensor", "context", None),
            P("dp", "tensor", "context"),
            P("dp", "tensor", "context"),
            P("dp", None),
            P("dp", None),
            P("context", None),
            P("dp", "context"),
        ),
        out_specs=P("context", "dp", "tensor"),
        check_vma=False,
    )
```

profile of v0, /device:TPU:0, one launch (start us, length us, event | category | flops | bytes accessed | tf_op | source)
XLA Modules:
  0.0 438.9 jit_solution(9843554968246785329)
XLA Ops:
  11.4 6.3 %all-to-all-start.2 = ((bf16[8,2,256]{2,1,0:T(2,128)(2,1)}), bf16[8,2,256]{2,1,0:T(2,128)(2,1)S(1)}, u32[]{:S(2)}, u32[]{:S(2)}) async-start(bf16[8,2,256]{2,1,0:T(2,128)(2,1)} %reshape.348), calls=%async_computation.2 | async-start | bytes 16384 | tf_op jit(solution)/shard_map/all_to_all | solution.py:123
  18.6 1.5 reshape_squeeze.22
  20.9 2.5 all-to-all-done.2
  23.3 3.3 all-to-all-start.5
  27.1 1.5 copy.69
  28.6 3.6 all-to-all-done.5
  32.2 3.6 all-to-all-start
  39.3 1.5 reshape_squeeze.25
  41.3 1.6 copy.75
  45.0 17.3 %all-to-all-done = bf16[16,8,4096]{2,1,0:T(8,128)(2,1)S(1)} async-done(((bf16[16,8,4096]{2,1,0:T(8,128)(2,1)}), bf16[16,8,4096]{2,1,0:T(8,128)(2,1)S(1)}, u32[]{:S(2)}, u32[]{:S(2)}) %all-to-all-start) | async-done | bytes 1048608 | tf_op jit(solution)/shard_map/all_to_all | solution.py:119
  62.2 3.6 all-to-all-start.3
  68.1 1.7 fusion.12
  69.8 2.3 reshape.310
  73.4 19.0 %all-to-all-done.3 = bf16[16,8,4096]{2,1,0:T(8,128)(2,1)S(1)} async-done(((bf16[16,8,4096]{2,1,0:T(8,128)(2,1)}), bf16[16,8,4096]{2,1,0:T(8,128)(2,1)S(1)}, u32[]{:S(2)}, u32[]{:S(2)}) %all-to-all-start.3) | async-done | bytes 1048608 | tf_op jit(solution)/shard_map/all_to_all | solution.py:120
  92.4 3.4 all-to-all-start.1
  100.0 9.4 %all-to-all-done.1 = bf16[16,2,4096]{2,1,0:T(2,128)(2,1)S(1)} async-done(((bf16[16,2,4096]{2,1,0:T(2,128)(2,1)}), bf16[16,2,4096]{2,1,0:T(2,128)(2,1)S(1)}, u32[]{:S(2)}, u32[]{:S(2)}) %all-to-all-start.1) | async-done | bytes 262176 | tf_op jit(solution)/shard_map/all_to_all | solution.py:121
  109.4 3.6 all-to-all-start.4
  114.2 12.0 %all-to-all-done.4 = bf16[16,2,4096]{2,1,0:T(2,128)(2,1)S(1)} async-done(((bf16[16,2,4096]{2,1,0:T(2,128)(2,1)}), bf16[16,2,4096]{2,1,0:T(2,128)(2,1)S(1)}, u32[]{:S(2)}, u32[]{:S(2)}) %all-to-all-start.4) | async-done | bytes 262176 | tf_op jit(solution)/shard_map/all_to_all | solution.py:122
  126.7 3.0 pad_maximum_fusion
  129.7 2.7 pad_maximum_fusion.1
  132.4 49.3 %while.16 = (s32[]{:T(128)}, f32[2,512,128]{2,1,0:T(8,128)S(1)}, f32[2,512,128]{2,1,0:T(8,128)}, s32[1024]{0:T(1024)S(1)}, s32[512]{0:T(512)S(1)}, /*index=5*/s3...) while((s32[]{:T(128)}, f32[2,512,128]{2,1,0:T(8,128)S(1)}, ...), condition=%wide.region_7.8_spmd.clone, body=%wide.region_6.7_spmd.clone.sunk | while | flops 541395456 | bytes 11179250 | solution.py:181
  133.8 1.6 exponential_select_fusion.2
  136.3 1.3 fusion.147
  139.1 1.6 exponential_select_fusion.2
  141.6 2.4 fusion.147
  145.4 1.6 exponential_select_fusion.2
  147.9 2.4 fusion.147
  151.7 1.6 exponential_select_fusion.2
  154.2 2.4 fusion.147
  158.0 1.6 exponential_select_fusion.2
  160.5 2.4 fusion.147
  164.2 1.6 exponential_select_fusion.2
  166.8 2.4 fusion.147
  170.5 1.6 exponential_select_fusion.2
  173.1 2.4 fusion.147
  176.8 1.6 exponential_select_fusion.2
  179.4 2.4 fusion.147
  184.6 17.8 %all_to_all.66 = bf16[8,2,16384]{2,1,0:T(2,128)(2,1)S(1)} all-to-all(bf16[8,2,16384]{2,1,0:T(2,128)(2,1)S(1)} %all_to_all.50), channel_id=1, replica_groups=mesh['dp'=2,'context'=8,'tensor'=2] {'context'}, dimensions={0} | all-to-all | bytes 1048576 | tf_op jit(solution)/shard_map/all_to_all | solution.py:191
  202.6 18.9 %copy.82 = bf16[1,512,4096]{1,0,2:T(2,128)(2,1)} copy(bf16[1,512,4096]{2,1,0:T(8,128)(2,1)} %all-gather.5.cloned.1.call-done) | data formatting | bytes 8388608 | tf_op jit(solution)/shard_map/all_gather | solution.py:196
  222.0 28.5 %reduce.7 = bf16[4096,512]{1,0:T(8,128)(2,1)} reduce(bf16[4096,1,512]{2,1,0:T(2,128)(2,1)} %bitcast.164, bf16[]{:T(256)} %broadcast.469), dimensions={1}, to_apply=%bitcast.122.reduce_sub_computation | reduce | bytes 8388610
  250.5 7.8 %reshape.346 = bf16[8,2,131072]{2,1,0:T(2,128)(2,1)} reshape(bf16[4096,512]{1,0:T(8,128)(2,1)} %reduce.7) | data formatting | bytes 8388608
  258.3 4.6 %all-to-all-start.7 = ((bf16[8,2,131072]{2,1,0:T(2,128)(2,1)}), bf16[8,2,131072]{2,1,0:T(2,128)(2,1)}, u32[]{:S(2)}, u32[]{:S(2)}) async-start(bf16[8,2,131072]{2,1,0:T(2,128)(2,1)} %reshape.346), calls=%async_computation.7 | async-start | bytes 8388608 | tf_op jit(solution)/shard_map/all_to_all | solution.py:197
  264.7 126.0 %all-to-all-done.7 = bf16[8,2,131072]{2,1,0:T(2,128)(2,1)} async-done(((bf16[8,2,131072]{2,1,0:T(2,128)(2,1)}), bf16[8,2,131072]{2,1,0:T(2,128)(2,1)}, u32[]{:S(2)}, u32[]{:S(2)}) %all-to-all-start.7) | async-done | bytes 4194336 | tf_op jit(solution)/shard_map/all_to_all | solution.py:197
  390.6 8.8 %reshape.347 = bf16[4096,1,512]{2,1,0:T(2,128)(2,1)} reshape(bf16[8,2,131072]{2,1,0:T(2,128)(2,1)} %all-to-all-done.7) | data formatting | bytes 8388608
  399.4 6.5 %copy.93 = bf16[1,512,4096]{1,2,0:T(8,128)(2,1)} copy(bf16[1,512,4096]{1,0,2:T(2,128)(2,1)} %bitcast.165) | data formatting | bytes 8388608
  405.9 6.4 %copy.83 = bf16[1,8,512,512]{3,2,1,0:T(8,128)(2,1)} copy(bf16[1,8,512,512]{2,3,1,0:T(8,128)(2,1)} %bitcast.168) | data formatting | bytes 8388608 | tf_op jit(solution)/shard_map/all_to_all | solution.py:197
  412.4 5.8 %fusion.16 = f32[512,512]{0,1:T(8,128)S(1)} fusion(bf16[4096,512]{1,0:T(8,128)(2,1)} %bitcast.169, bf16[1,4096,512]{2,1,0:T(8,128)(2,1)} %all-gather.3.cloned.1.call-done), kind=kOutput, calls=%fused_computation.34 | convolution fusion | flops 2147483648 | bytes 9437184 | tf_op jit(solution)/shard_map/td,tc->dc/dot_general | solution.py:199
  420.0 10.5 %all_to_all.67 = bf16[1,4,128,512]{3,1,0,2:T(4,128)(2,1)S(1)} all-to-all(bf16[1,4,128,512]{3,1,0,2:T(4,128)(2,1)S(1)} %copy.85), channel_id=1, replica_groups=mesh['dp'=2,'context'=8,'tensor'=2] {'dp'}, dimensions={2} | all-to-all | bytes 1048576 | tf_op jit(solution)/shard_map/all_to_all | solution.py:214
  (169 shorter events, 47.6 us)
Async XLA Ops:
  11.4 11.9 %all-to-all-start.2 = ((bf16[8,2,256]{2,1,0:T(2,128)(2,1)}), bf16[8,2,256]{2,1,0:T(2,128)(2,1)S(1)}, u32[]{:S(2)}, u32[]{:S(2)}) async-start(bf16[8,2,256]{2,1,0:T(2,128)(2,1)} %reshape.348), calls=%async_computation.2 | async-start | bytes 16384 | tf_op jit(solution)/shard_map/all_to_all | solution.py:123
  23.3 8.9 %all-to-all-start.5 = ((bf16[8,2,256]{2,1,0:T(2,128)(2,1)}), bf16[8,2,256]{2,1,0:T(2,128)(2,1)S(1)}, u32[]{:S(2)}, u32[]{:S(2)}) async-start(bf16[8,2,256]{2,1,0:T(2,128)(2,1)} %reshape.350), calls=%async_computation.5 | async-start | bytes 16384 | tf_op jit(solution)/shard_map/all_to_all | solution.py:124
  28.6 7.9 %copy-start.4 = (s32[1,10]{1,0:T(1,128)S(1)}, s32[1,10]{1,0:T(1,128)}, u32[]{:S(2)}) copy-start(s32[1,10]{1,0:T(1,128)} %param.20) | copy-start | bytes 124
  28.6 8.6 %copy-start.3 = (s32[1,128]{1,0:T(1,128)S(1)}, s32[1,128]{1,0:T(1,128)}, u32[]{:S(2)}) copy-start(s32[1,128]{1,0:T(1,128)} %param.21) | copy-start | bytes 1540
  28.6 9.3 %copy-start = (bf16[1,2,512,128]{3,2,1,0:T(8,128)(2,1)S(1)}, bf16[1,2,512,128]{3,2,1,0:T(8,128)(2,1)}, u32[]{:S(2)}) copy-start(bf16[1,2,512,128]{3,2,1,0:T(8,128)(2,1)} %param.15) | copy-start | bytes 786436
  32.2 30.1 %all-to-all-start = ((bf16[16,8,4096]{2,1,0:T(8,128)(2,1)}), bf16[16,8,4096]{2,1,0:T(8,128)(2,1)S(1)}, u32[]{:S(2)}, u32[]{:S(2)}) async-start(bf16[16,8,4096]{2,1,0:T(8,128)(2,1)} %copy.69), calls=%async_computation | async-start | bytes 2097152 | tf_op jit(solution)/shard_map/all_to_all | solution.py:119
  35.7 166.9 %all-gather.5.cloned.1.call-start = ((), (), s32[]{:S(2)}) async-start(), calls=%async_computation.10 | async-start | bytes 6291456 | tf_op jit(solution)/shard_map/all_gather | solution.py:196
  40.8 2.0 copy-start.1
  62.2 30.2 %all-to-all-start.3 = ((bf16[16,8,4096]{2,1,0:T(8,128)(2,1)}), bf16[16,8,4096]{2,1,0:T(8,128)(2,1)S(1)}, u32[]{:S(2)}, u32[]{:S(2)}) async-start(bf16[16,8,4096]{2,1,0:T(8,128)(2,1)} %copy.75), calls=%async_computation.3 | async-start | bytes 2097152 | tf_op jit(solution)/shard_map/all_to_all | solution.py:120
  66.7 46.4 %collective-permute-start.1 = (bf16[8,512]{1,0:T(8,128)(2,1)S(1)}, bf16[8,512]{1,0:T(8,128)(2,1)S(1)}, u32[]{:S(2)}, u32[]{:S(2)}) collective-permute-start(bf16[8,512]{1,0:T(8,128)(2,1)S(1)} %squeeze_reshape.6), channel_id=1, source_target_pairs={{2,0},{4,2},{6,4},{8,6},{10,8},{12,10},{14,12},{3,1},{5,3},{7,5},{... | collective-permute-start | bytes 24584 | tf_op jit(solution)/shard_map/ppermute | solution.py:18
  72.1 54.6 %collective-permute-start = (bf16[8,512,128]{2,1,0:T(8,128)(2,1)}, bf16[8,512,128]{2,1,0:T(8,128)(2,1)}, u32[]{:S(2)}, u32[]{:S(2)}) collective-permute-start(bf16[8,512,128]{2,1,0:T(8,128)(2,1)} %reshape.310), channel_id=1, source_target_pairs={{2,0},{4,2},{6,4},{8,6},{10,8},{12,10},{14,12},{3,1},{5,3},{7,5},{... | collective-permute-start | bytes 3145736 | tf_op jit(solution)/shard_map/ppermute | solution.py:18
  92.4 17.0 %all-to-all-start.1 = ((bf16[16,2,4096]{2,1,0:T(2,128)(2,1)}), bf16[16,2,4096]{2,1,0:T(2,128)(2,1)S(1)}, u32[]{:S(2)}, u32[]{:S(2)}) async-start(bf16[16,2,4096]{2,1,0:T(2,128)(2,1)} %copy.71), calls=%async_computation.1 | async-start | bytes 524288 | tf_op jit(solution)/shard_map/all_to_all | solution.py:121
  97.1 32.6 %collective-permute-start.2 = (bf16[8,512,128]{2,1,0:T(8,128)(2,1)S(1)}, bf16[8,512,128]{2,1,0:T(8,128)(2,1)}, u32[]{:S(2)}, u32[]{:S(2)}) collective-permute-start(bf16[8,512,128]{2,1,0:T(8,128)(2,1)S(1)} %reshape.312), channel_id=1, source_target_pairs={{2,0},{4,2},{6,4},{8,6},{10,8},{12,10},{14,12},{3,1},{5,3},{7,5},{... | collective-permute-start | bytes 3145736 | tf_op jit(solution)/shard_map/ppermute | solution.py:18
  98.7 14.3 %collective-permute-start.3 = (bf16[8,512]{1,0:T(8,128)(2,1)S(1)}, bf16[8,512]{1,0:T(8,128)(2,1)S(1)}, u32[]{:S(2)}, u32[]{:S(2)}) collective-permute-start(bf16[8,512]{1,0:T(8,128)(2,1)S(1)} %squeeze_reshape.7), channel_id=1, source_target_pairs={{2,0},{4,2},{6,4},{8,6},{10,8},{12,10},{14,12},{3,1},{5,3},{7,5},{... | collective-permute-start | bytes 24584 | tf_op jit(solution)/shard_map/ppermute | solution.py:18
  109.4 16.8 %all-to-all-start.4 = ((bf16[16,2,4096]{2,1,0:T(2,128)(2,1)}), bf16[16,2,4096]{2,1,0:T(2,128)(2,1)S(1)}, u32[]{:S(2)}, u32[]{:S(2)}) async-start(bf16[16,2,4096]{2,1,0:T(2,128)(2,1)} %copy.77), calls=%async_computation.4 | async-start | bytes 524288 | tf_op jit(solution)/shard_map/all_to_all | solution.py:122
  258.3 132.3 %all-to-all-start.7 = ((bf16[8,2,131072]{2,1,0:T(2,128)(2,1)}), bf16[8,2,131072]{2,1,0:T(2,128)(2,1)}, u32[]{:S(2)}, u32[]{:S(2)}) async-start(bf16[8,2,131072]{2,1,0:T(2,128)(2,1)} %reshape.346), calls=%async_computation.7 | async-start | bytes 8388608 | tf_op jit(solution)/shard_map/all_to_all | solution.py:197
  262.9 1.7 copy-start.2
  262.9 1.7 copy-start.5
  262.9 149.4 %all-gather.3.cloned.1.call-start = ((), (), s32[]{:S(2)}) async-start(), calls=%async_computation.9 | async-start | bytes 4718592 | tf_op jit(solution)/shard_map/all_gather | solution.py:202
Sparse Core Ops, SparseCore 0:
  38.1 58.2 all-gather.4
Sparse Core Ops, SparseCore 1:
  265.0 81.5 all-gather.2
where the time goes:
time: 442 us; the launch traced here: 439 us
  waiting for transfers between devices  190 us (43%)
  local copies, waits for them, and re-layouts  79 us (18%)
  matrix products  50.4 us (11%)
  other arithmetic  41.2 us (9%)
  starting transfers between devices  33.8 us (8%)
  blocking collectives  28.2 us (6%)
  between operations  15.3 us (3%)
    all_to_all x1, waiting for transfers between devices, per_device(): lax.all_to_all(full_input, 'context', split_axis=2, concat_axis=1, tiled=...  126 us
    unnamed x4, other arithmetic  29.1 us
    unnamed x21, local copies, waits for them, and re-layouts  25.8 us
    all_to_all x1, waiting for transfers between devices, per_device(): lax.all_to_all(pack(out_grad), 'context', split_axis=0, concat_axis=0, ti...  19 us
    all_gather x1, local copies, waits for them, and re-layouts, per_device(): full_input = lax.all_gather(layer_input, 'tensor', axis=2, tiled=True)  18.9 us
    dot_general x8, matrix products, block_grads(): jnp.einsum('ghqk,ghqd->gkd', probs.astype(jnp.bfloat16), grad_blk, prefer...  18 us
    all_to_all x1, blocking collectives, per_device(): lax.all_to_all(outgoing, 'context', split_axis=0, concat_axis=0, tiled=True)  17.8 us
    all_to_all x1, waiting for transfers between devices, per_device(): lax.all_to_all(pack(queries), 'context', split_axis=0, concat_axis=0, til...  17.3 us
  transfers between devices with their start and end apart: 13, of which 7 were waited for; matrix products, arithmetic and copies ran while one was open for 23% of the time, Pallas kernels for 0%

commit v1 on v0

v1 whole, which is shorter than its diff:
```python
import functools

import jax
import jax.numpy as jnp
from jax import lax
from jax.experimental import pallas as pl
from jax.experimental.pallas import tpu as pltpu
from jax.sharding import PartitionSpec as P

HD = 128
GROUP = 4
BLK = 32
PAD = 128
HB = 128
MESH = pl.DeviceIdType.MESH
STEP = 2 * PAD
VMEM_MAX = 56 * 1024 * 1024


def hadamard_signs(table_size):
    index_row = jnp.arange(table_size, dtype=jnp.int32)
    common = jnp.bitwise_and(index_row[:, None], index_row[None, :])
    parity = jnp.zeros((table_size, table_size), jnp.int32)
    for bit_pos in range(table_size.bit_length() - 1):
        parity = parity + jnp.bitwise_and(jnp.right_shift(common, bit_pos), 1)
    return (1 - 2 * jnp.bitwise_and(parity, 1)).astype(jnp.float32)


def attention_kernel(
    order_ref,
    docs_ref,
    query_ref,
    grad_ref,
    lse_ref,
    dots_ref,
    kv_ref,
    out_ref,
    kv_sorted,
    acc,
):
    groups, kv_heads, local_tokens, width = kv_ref.shape
    slots = local_tokens // BLK
    stored = groups * slots
    me = lax.axis_index("context")
    scale = HD ** (-0.5)
    rows = GROUP * BLK

    kv_sorted[:, :PAD, :] = jnp.zeros((kv_heads, PAD, width), kv_sorted.dtype)
    acc[...] = jnp.zeros_like(acc)

    @pl.loop(0, groups)
    def _(owner):
        for slot in range(slots):
            place = pl.multiple_of(PAD + order_ref[0, owner * slots + slot] * BLK, BLK)
            for head in range(kv_heads):
                kv_sorted[head, pl.ds(place, BLK), :] = kv_ref[
                    owner, head, pl.ds(slot * BLK, BLK), :
                ]

    key_iota = lax.broadcasted_iota(jnp.int32, (STEP, rows), 0)
    query_iota = lax.rem(lax.broadcasted_iota(jnp.int32, (STEP, rows), 1), BLK)

    @pl.loop(0, slots)
    def _(slot):
        block = order_ref[0, me * slots + slot]
        unit = block // (PAD // BLK)
        total = jnp.int32(0)
        start = jnp.int32(0)
        for doc in range(docs_ref.shape[1]):
            start = jnp.where(total <= unit, total, start)
            total = total + docs_ref[0, doc]
        query_pos = query_iota + block * BLK

        @pl.loop(0, (unit - start) // 2 + 1)
        def _(part):
            low_unit = unit - 1 - 2 * part
            place = pl.multiple_of((low_unit + 1) * PAD, PAD)
            key_pos = key_iota + low_unit * PAD
            live = (key_pos <= query_pos) & (key_pos >= start * PAD)
            for head in range(kv_heads):
                span = pl.ds(pl.multiple_of(slot * BLK, BLK), BLK)
                heads = pl.ds(head * GROUP, GROUP)
                query = query_ref[heads, span, :].reshape(rows, HD)
                grad = grad_ref[heads, span, :].reshape(rows, HD)
                key = kv_sorted[head, pl.ds(place, STEP), :HD]
                value = kv_sorted[head, pl.ds(place, STEP), HD:]
                lse = lse_ref[slot, head : head + 1, :]
                dots = dots_ref[slot, head : head + 1, :]
                nt = (((1,), (1,)), ((), ()))
                scores = lax.dot_general(key, query, nt, preferred_element_type=jnp.float32)
                dprobs = lax.dot_general(value, grad, nt, preferred_element_type=jnp.float32)
                probs = jnp.where(live, jnp.exp(scores * scale - lse), 0.0)
                dscores = (probs * (dprobs - dots)).astype(jnp.bfloat16)
                acc[head, pl.ds(place, STEP), :HD] += jnp.dot(
                    dscores, query, preferred_element_type=jnp.float32
                )
                acc[head, pl.ds(place, STEP), HD:] += jnp.dot(
                    probs.astype(jnp.bfloat16), grad, preferred_element_type=jnp.float32
                )

    @pl.loop(0, groups)
    def _(owner):
        for slot in range(slots):
            place = pl.multiple_of(PAD + order_ref[0, owner * slots + slot] * BLK, BLK)
            for head in range(kv_heads):
                low = head * width
                piece = acc[head, pl.ds(place, BLK), :]
                out_ref[owner, pl.ds(slot * BLK, BLK), low : low + HD] = (
                    piece[:, :HD] * scale
                ).astype(out_ref.dtype)
                out_ref[owner, pl.ds(slot * BLK, BLK), low + HD : low + width] = piece[
                    :, HD:
                ].astype(out_ref.dtype)


def attention(order, docs, queries, out_grad, lse, dots, kv_all):
    groups, kv_heads, local_tokens, width = kv_all.shape
    total = groups * local_tokens
    smem = pl.BlockSpec(memory_space=pltpu.SMEM)
    vmem = pl.BlockSpec(memory_space=pltpu.VMEM)
    return pl.pallas_call(
        attention_kernel,
        out_shape=jax.ShapeDtypeStruct(
            (groups, local_tokens, kv_heads * width), jnp.bfloat16
        ),
        in_specs=[smem, smem] + [vmem] * 5,
        out_specs=vmem,
        scratch_shapes=[
            pltpu.VMEM((kv_heads, PAD + total, width), jnp.bfloat16),
            pltpu.VMEM((kv_heads, PAD + total, width), jnp.float32),
        ],
        compiler_params=pltpu.CompilerParams(vmem_limit_bytes=VMEM_MAX),
        cost_estimate=pl.CostEstimate(
            flops=4 * 10**9, bytes_accessed=14 * 2**20, transcendentals=2**21
        ),
    )(order, docs, queries, out_grad, lse, dots, kv_all)


def ring_sum(out_at, own_at, parts):
    out_at[...] = functools.reduce(
        lambda a, b: a + b, [r[...].astype(jnp.float32) for r in [own_at] + parts]
    ).astype(out_at.dtype)


def line_stage(n, pos, device, source, target, send, recv, sems, looped):
    def copy(side, step, src):
        return pltpu.make_async_remote_copy(
            src_ref=src,
            dst_ref=recv.at[side, step],
            send_sem=sems.at[side, 0, step],
            recv_sem=sems.at[side, 1, step],
            device_id=device(1 if side == 0 else -1),
            device_id_type=MESH,
        )

    def add(out_at, own_at, parts):
        looped(out_at, own_at, parts)

    for step in range(n - 1):
        for side in (0, 1):
            place = pos if side == 0 else n - 1 - pos
            away = n - 1 - step
            dest = pos + away if side == 0 else pos - away

            @pl.when(place == 0)
            def _(side=side, step=step, dest=dest):
                copy(side, step, source(dest)).start()

            if step > 0:

                @pl.when((place >= 1) & (place <= step))
                def _(side=side, step=step, dest=dest):
                    copy(side, step - 1, send.at[side, step - 1]).wait_recv()
                    add(send.at[side, step], source(dest), [recv.at[side, step - 1]])
                    copy(side, step, send.at[side, step]).start()

    last = n - 2

    def arrived(side):
        copy(side, last, send.at[side, last]).wait_recv()

    if n > 2:

        @pl.when((pos >= 1) & (pos <= n - 2))
        def _():
            arrived(0)
            arrived(1)
            add(target, source(pos), [recv.at[0, last], recv.at[1, last]])

    @pl.when(pos == 0)
    def _():
        arrived(1)
        add(target, source(pos), [recv.at[1, last]])

    @pl.when(pos == n - 1)
    def _():
        arrived(0)
        add(target, source(pos), [recv.at[0, last]])

    for step in range(n - 1):
        for side in (0, 1):
            place = pos if side == 0 else n - 1 - pos

            @pl.when(place <= step)
            def _(side=side, step=step):
                copy(side, step, send.at[side, step]).wait_send()


def add_rows(out_at, own_at, parts):
    lead = out_at.shape[0]

    @pl.loop(0, lead)
    def _(i):
        ring_sum(out_at.at[i], own_at.at[i], [p.at[i] for p in parts])


def neighbours_barrier(lines):
    barrier = pltpu.get_barrier_semaphore()
    count = jnp.int32(0)
    for n, pos, device in lines:

        @pl.when(pos >= 1)
        def _(device=device):
            pl.semaphore_signal(barrier, inc=1, device_id=device(-1), device_id_type=MESH)

        @pl.when(pos <= n - 2)
        def _(device=device):
            pl.semaphore_signal(barrier, inc=1, device_id=device(1), device_id_type=MESH)

        count = count + jnp.where(pos >= 1, 1, 0) + jnp.where(pos <= n - 2, 1, 0)
    pl.semaphore_wait(barrier, count)


def context_lines(chips):
    me = lax.axis_index("context")
    chip, core = me // 2, lax.rem(me, 2)
    core_line = (2, core, lambda d: {"context": me + d})
    chip_line = (chips, chip, lambda d: {"context": me + 2 * d})
    return core_line, chip_line


def token_sum_kernel(part_ref, out_ref, half, send_a, recv_a, sem_a, send_b, recv_b, sem_b):
    chips = part_ref.shape[0]
    core_line, chip_line = context_lines(chips)
    neighbours_barrier([core_line, chip_line])
    line_stage(
        *core_line, lambda d: part_ref.at[:, d], half, send_a, recv_a, sem_a, add_rows
    )
    line_stage(
        *chip_line, lambda d: half.at[d], out_ref, send_b, recv_b, sem_b, add_rows
    )


def stage_scratch(n, shape):
    return [
        pltpu.VMEM((2, n - 1) + shape, jnp.bfloat16),
        pltpu.VMEM((2, n - 1) + shape, jnp.bfloat16),
        pltpu.SemaphoreType.DMA((2, 2, n - 1)),
    ]


def token_sum(parts):
    chips, cores, slabs, rows, cols = parts.shape
    vmem = pl.BlockSpec(memory_space=pltpu.VMEM)
    return pl.pallas_call(
        token_sum_kernel,
        out_shape=jax.ShapeDtypeStruct((slabs, rows, cols), jnp.bfloat16),
        in_specs=[vmem],
        out_specs=vmem,
        scratch_shapes=[pltpu.VMEM((chips, slabs, rows, cols), jnp.bfloat16)]
        + stage_scratch(cores, (chips, slabs, rows, cols))
        + stage_scratch(chips, (slabs, rows, cols)),
        compiler_params=pltpu.CompilerParams(
            collective_id=1, has_side_effects=True, vmem_limit_bytes=VMEM_MAX
        ),
        cost_estimate=pl.CostEstimate(
            flops=10**7, bytes_accessed=5 * 2**20, transcendentals=0
        ),
    )(parts)


def final_sum_kernel(
    part_ref,
    out_ref,
    half,
    quarter,
    send_a,
    recv_a,
    sem_a,
    send_b,
    recv_b,
    sem_b,
    send_c,
    recv_c,
    sem_c,
):
    chips, _, blocks, copies, rows, cols = part_ref.shape
    core_line, chip_line = context_lines(chips)
    mine = lax.axis_index("dp")
    dp_line = (copies, mine, lambda d: {"dp": mine + d})
    neighbours_barrier([core_line, dp_line, chip_line])
    line_stage(
        *core_line, lambda d: part_ref.at[:, d], half, send_a, recv_a, sem_a, add_rows
    )
    line_stage(
        *dp_line, lambda d: half.at[:, :, d], quarter, send_b, recv_b, sem_b, add_rows
    )
    line_stage(
        *chip_line, lambda d: quarter.at[d], out_ref, send_c, recv_c, sem_c, add_rows
    )


def final_sum(parts):
    chips, cores, blocks, copies, rows, cols = parts.shape
    vmem = pl.BlockSpec(memory_space=pltpu.VMEM)
    return pl.pallas_call(
        final_sum_kernel,
        out_shape=jax.ShapeDtypeStruct((blocks, rows, cols), jnp.float32),
        in_specs=[vmem],
        out_specs=vmem,
        scratch_shapes=[
            pltpu.VMEM((chips, blocks, copies, rows, cols), jnp.bfloat16),
            pltpu.VMEM((chips, blocks, rows, cols), jnp.bfloat16),
        ]
        + stage_scratch(cores, (chips, blocks, copies, rows, cols))
        + stage_scratch(copies, (chips, blocks, rows, cols))
        + stage_scratch(chips, (blocks, rows, cols)),
        compiler_params=pltpu.CompilerParams(
            collective_id=2, has_side_effects=True, vmem_limit_bytes=VMEM_MAX
        ),
        cost_estimate=pl.CostEstimate(
            flops=10**7, bytes_accessed=5 * 2**20, transcendentals=0
        ),
    )(parts)


def per_device(
    layer_input,
    queries,
    key_states,
    value_states,
    out_grad,
    log_sums,
    grad_dots,
    doc_stretches,
    stretch_order,
    sign_vector,
    exponents,
):
    heads, local_tokens = queries.shape[1], queries.shape[2]
    local_kv = key_states.shape[1]
    local_cols = 2 * local_kv * HD
    groups = lax.axis_size("context")
    copies = lax.axis_size("dp")
    chips = groups // 2
    slots = local_tokens // BLK

    kv_own = jnp.concatenate([key_states[0], value_states[0]], axis=-1)
    kv_all = lax.all_gather(kv_own, "context", axis=0, tiled=False)

    factor = 1.0 / jnp.left_shift(jnp.int32(1), exponents[0]).astype(jnp.float32)
    signs = (sign_vector.astype(jnp.float32) * factor[:, None]).astype(jnp.bfloat16)
    signs_all = lax.all_gather(signs, "context", axis=0, tiled=True)
    local_blocks = layer_input.shape[2] // HB
    signs_own = lax.dynamic_slice_in_dim(
        signs_all, lax.axis_index("tensor") * local_blocks, local_blocks, 0
    )
    turn = hadamard_signs(HB)[None] * signs_own.astype(jnp.float32)[:, None, :]
    rotated_input = (
        jnp.einsum(
            "bij,tbj->bit",
            turn.astype(jnp.bfloat16),
            layer_input[0].reshape(local_tokens, local_blocks, HB),
            preferred_element_type=jnp.float32,
        )
        * float(HB) ** (-0.5)
    ).astype(jnp.bfloat16)
    rotated_all = lax.all_gather(
        rotated_input.reshape(local_blocks * HB, local_tokens), "tensor", axis=0, tiled=True
    )

    def row_stats(stat):
        split = stat[0].astype(jnp.float32).reshape(local_kv, GROUP, slots, BLK)
        return jnp.transpose(split, (2, 0, 1, 3)).reshape(slots, local_kv, GROUP * BLK)

    parts = attention(
        stretch_order,
        doc_stretches,
        queries[0],
        out_grad[0],
        row_stats(log_sums),
        row_stats(grad_dots),
        kv_all,
    )
    slabs = 4
    kv_grad = token_sum(
        parts.reshape(chips, 2, slabs, local_tokens // slabs, local_cols)
    ).reshape(local_tokens, local_cols)
    member = jnp.dot(rotated_all, kv_grad, preferred_element_type=jnp.float32).astype(
        jnp.bfloat16
    )
    own_blocks = sign_vector.shape[0]
    return final_sum(
        member.reshape(chips, 2, own_blocks, copies, HB // copies, local_cols)
    )


def solution(mesh):
    return jax.shard_map(
        per_device,
        mesh=mesh,
        in_specs=(
            P("dp", "context", "tensor"),
            P("dp", "tensor", "context", None),
            P("dp", "tensor", "context", None),
            P("dp", "tensor", "context", None),
            P("dp", "tensor", "context", None),
            P("dp", "tensor", "context"),
            P("dp", "tensor", "context"),
            P("dp", None),
            P("dp", None),
            P("context", None),
            P("dp", "context"),
        ),
        out_specs=P("context", "dp", "tensor"),
        check_vma=False,
    )
```

time: 442 us -> 197 us (0.45)
  waiting for transfers between devices: 190 us -> 30 us
  Pallas kernels: 0 us -> 122 us
  local copies, waits for them, and re-layouts: 79 us -> 5.72 us
  matrix products: 50.4 us -> 9.47 us
  other arithmetic: 41.2 us -> 2.05 us
  starting transfers between devices: 33.8 us -> 0.04 us
  blocking collectives: 28.2 us -> 13.5 us
    all_to_all x7 -> x0, waiting for transfers between devices: 190 us -> none  [the longest x1 126 us: per_device(): lax.all_to_all(full_input, 'context', split_axis=2, concat_axis=1, tiled=...]
    pallas_call x0 -> x3, Pallas kernels: none -> 122 us  [the longest x1 53.6 us: final_sum(): pl.pallas_call(final_sum_kernel, out_shape=jax.ShapeDtypeStruct((blocks,...]
    dot_general x40 -> x2, matrix products: 50.4 us -> 9.47 us  [the longest x1 6.73 us: per_device(): jnp.dot(rotated_all, kv_grad, preferred_element_type=jnp.float32)]
    all_gather x2, waiting for transfers between devices: 0.02 us -> 30 us  [the longest x1 30 us: per_device(): kv_all = lax.all_gather(kv_own, 'context', axis=0, tiled=False)]
    unnamed x4 -> x1, other arithmetic: 29.1 us -> 0.07 us
    all_to_all x7 -> x0, starting transfers between devices: 28.3 us -> none  [the longest x1 6.33 us: per_device(): lax.all_to_all(pack(log_sums), 'context', split_axis=0, concat_axis=0, ti...]
    all_to_all x2 -> x0, blocking collectives: 28.2 us -> none  [the longest x1 17.8 us: per_device(): lax.all_to_all(outgoing, 'context', split_axis=0, concat_axis=0, tiled=True)]
    unnamed x21 -> x10, local copies, waits for them, and re-layouts: 25.8 us -> 4.09 us
  transfers between devices with their start and end apart: 13 -> 2, of which waited for: 7 -> 1; matrix products, arithmetic and copies ran while one was open for 23% -> 3% of each run, Pallas kernels for 0% -> 35%
where the time goes in v1:
time: 197 us; the launch traced here: 196 us
  Pallas kernels  122 us (62%)
  waiting for transfers between devices  30 us (15%)
  blocking collectives  13.5 us (7%)
  between operations  13.5 us (7%)
  matrix products  9.47 us (5%)
  local copies, waits for them, and re-layouts  5.72 us (3%)
  other arithmetic  2.05 us (1%)
    pallas_call x1, Pallas kernels, final_sum(): pl.pallas_call(final_sum_kernel, out_shape=jax.ShapeDtypeStruct((blocks,...  53.6 us
    pallas_call x1, Pallas kernels, token_sum(): pl.pallas_call(token_sum_kernel, out_shape=jax.ShapeDtypeStruct((slabs, r...  50 us
    all_gather x1, waiting for transfers between devices, per_device(): kv_all = lax.all_gather(kv_own, 'context', axis=0, tiled=False)  30 us
    pallas_call x1, Pallas kernels, attention(): pl.pallas_call(attention_kernel, out_shape=jax.ShapeDtypeStruct((groups,...  18.2 us
    all_gather x1, blocking collectives, per_device(): signs_all = lax.all_gather(signs, 'context', axis=0, tiled=True)  13.5 us
    dot_general x1, matrix products, per_device(): jnp.dot(rotated_all, kv_grad, preferred_element_type=jnp.float32)  6.73 us
    unnamed x10, local copies, waits for them, and re-layouts  4.09 us
  transfers between devices with their start and end apart: 2, of which 1 were waited for; matrix products, arithmetic and copies ran while one was open for 3% of the time, Pallas kernels for 35%

profile of v1, /device:TPU:0, one launch (start us, length us, event | category | flops | bytes accessed | tf_op | source)
XLA Modules:
  0.0 196.1 jit_solution(2857778311699848335)
XLA Ops:
  6.5 0.0 copy-start.3
  6.5 0.0 copy-start.2
  6.5 0.0 all-gather.7.cloned.1.call-start
  6.5 1.9 pad_maximum_fusion
  8.4 0.0 all-gather.7.cloned.1.call-update
  8.5 0.0 all-gather.5.cloned.1.call-start
  8.5 2.2 %copy.18 = bf16[64,8,16,128]{3,2,1,0:T(8,128)(2,1)S(1)} copy(bf16[64,8,16,128]{3,1,2,0:T(8,128)(2,1)} %bitcast.29) | data formatting | bytes 4194304
  10.7 0.0 copy-start
  10.7 0.0 copy-start.1
  10.8 0.0 copy-done.3
  10.8 0.0 copy-done.2
  10.8 0.1 fusion.3
  10.9 13.5 %all-gather.1 = bf16[8,4,128]{2,1,0:T(4,128)(2,1)S(1)} all-gather(bf16[1,4,128]{2,1,0:T(4,128)(2,1)S(1)} %fusion.3), channel_id=1, replica_groups=mesh['dp'=2,'context'=8,'tensor'=2] {'context'}, dimensions={0}, use_global_device_ids=true | all-gather | bytes 9216 | tf_op jit(solution)/shard_map/all_gather | solution.py:363
  24.4 0.1 subtract_convert_fusion
  24.5 2.7 %multiply_convert_fusion = bf16[16,128,512]{2,1,0:T(8,128)(2,1)} fusion(bf16[512,16,128]{2,1,0:T(8,128)(2,1)S(1)} %bitcast.26, f32[16,128]{1,0:T(8,128)S(1)} %dynamic-slice_convert_fusion, f32[128,128]{1,0:T(8,128)S(1)} %subtract_convert_fusion), kind=kOutput, calls=%fused_computation.1 | convolution fusion | flops 271056896 | bytes 4268032 | tf_op jit(solution)/shard_map/bij,tbj->bit/dot_general | solution.py:370
  27.2 0.0 all-gather.5.cloned.1.call-update
  27.2 0.0 copy-done
  27.2 0.1 reshape.94
  27.3 0.7 reshape.88.lse_ref
  28.1 0.0 copy-done.1
  28.1 0.1 reshape.96
  28.2 0.7 reshape.90.dots_ref
  28.9 30.0 %all-gather.7.cloned.1.call-done = bf16[16,512,256]{2,1,0:T(8,128)(2,1)} async-done(((bf16[2,512,256]{2,1,0:T(8,128)(2,1)}), bf16[16,512,256]{2,1,0:T(8,128)(2,1)}) %all-gather.7.cloned.1.call-update) | async-done | bytes 4194320 | tf_op jit(solution)/shard_map/all_gather | solution.py:359
  58.9 18.2 %shard_map.109 = bf16[8,512,512]{2,1,0:T(8,128)(2,1)} custom-call(s32[1,128]{1,0:T(1,128)} %order_ref.1, s32[1,10]{1,0:T(1,128)} %docs_ref.1, bf16[8,512,128]{2,1,0:T(8,128)(2,1)} %bitcast.37, bf16[8,512,128]{2,1,0:T(8,128)(2,1)} %bitcast.38, f32[16,2,128]{2,1,0:T(2,128)} %reshape.88.lse_ref, f32[16,2,128]{2,1,0:T(2,128)} %reshape.90.dots_ref, ...), custom_call_target="tpu_custom_call" | custom-call | flops 4000000000 | bytes 14680064 | tf_op jit(solution)/shard_map/pallas_call | solution.py:121
  77.0 50.0 %shard_map.110 = bf16[4,128,512]{2,1,0:T(8,128)(2,1)} custom-call(bf16[4,2,4,128,512]{4,3,2,1,0:T(8,128)(2,1)} %bitcast.27), custom_call_target="tpu_custom_call" | custom-call | flops 10000000 | bytes 5242880 | tf_op jit(solution)/shard_map/pallas_call | solution.py:265
  127.0 0.0 all-gather.5.cloned.1.call-done
  127.0 6.7 %convolution_convert_fusion = bf16[4096,512]{1,0:T(8,128)(2,1)} fusion(bf16[4096,512]{1,0:T(8,128)(2,1)} %all-gather.5.cloned.1.call-done, bf16[512,512]{1,0:T(8,128)(2,1)} %bitcast.30), kind=kOutput, calls=%fused_computation | convolution fusion | flops 2149580800 | bytes 8912896 | tf_op jit(solution)/shard_map/dot_general | solution.py:399
  133.8 53.6 %shard_map.111 = f32[4,64,512]{2,1,0:T(8,128)} custom-call(bf16[4,2,4,2,64,512]{5,4,3,2,1,0:T(8,128)(2,1)} %bitcast.28), custom_call_target="tpu_custom_call" | custom-call | flops 10000000 | bytes 5242880 | tf_op jit(solution)/shard_map/pallas_call | solution.py:316
  187.4 1.9 copy.26
  (4 shorter events, 0.1 us)
Async XLA Ops:
  6.5 4.2 %copy-start.3 = (s32[1,4]{1,0:T(1,128)S(1)}, s32[1,4]{1,0:T(1,128)}, u32[]{:S(2)}) copy-start(s32[1,4]{1,0:T(1,128)} %param.21) | copy-start | bytes 52
  6.5 4.2 %copy-start.2 = (s32[4,128]{1,0:T(4,128)S(1)}, s32[4,128]{1,0:T(4,128)}, u32[]{:S(2)}) copy-start(s32[4,128]{1,0:T(4,128)} %param.20) | copy-start | bytes 6148
  6.5 52.3 %all-gather.7.cloned.1.call-start = ((), (), s32[]{:S(2)}) async-start(), calls=%async_computation.1 | async-start | bytes 4718592 | tf_op jit(solution)/shard_map/all_gather | solution.py:359
  8.5 118.6 %all-gather.5.cloned.1.call-start = ((), (), s32[]{:S(2)}) async-start(), calls=%async_computation | async-start | bytes 6291456 | tf_op jit(solution)/shard_map/all_gather | solution.py:378
  10.7 16.5 %copy-start = (bf16[1,8,512]{2,1,0:T(8,128)(2,1)S(1)}, bf16[1,8,512]{2,1,0:T(8,128)(2,1)}, u32[]{:S(2)}) copy-start(bf16[1,8,512]{2,1,0:T(8,128)(2,1)} %param.16) | copy-start | bytes 24580
  10.7 17.3 %copy-start.1 = (bf16[1,8,512]{2,1,0:T(8,128)(2,1)S(1)}, bf16[1,8,512]{2,1,0:T(8,128)(2,1)}, u32[]{:S(2)}) copy-start(bf16[1,8,512]{2,1,0:T(8,128)(2,1)} %param.17) | copy-start | bytes 24580
Sparse Core Ops, SparseCore 0:
  9.0 49.8 all-gather.6
  60.4 55.5 all-gather.4

commit v2 on v1

--- a/solution.py
+++ b/solution.py
@@ -38,9 +38,9 @@
     kv_sorted,
     acc,
 ):
-    groups, kv_heads, local_tokens, width = kv_ref.shape
+    groups, kv_heads, _, width = kv_ref.shape
+    local_tokens = query_ref.shape[1]
     slots = local_tokens // BLK
-    stored = groups * slots
     me = lax.axis_index("context")
     scale = HD ** (-0.5)
     rows = GROUP * BLK
@@ -104,24 +104,26 @@
             place = pl.multiple_of(PAD + order_ref[0, owner * slots + slot] * BLK, BLK)
             for head in range(kv_heads):
                 low = head * width
+                half, row = divmod(slot * BLK, local_tokens // 2)
                 piece = acc[head, pl.ds(place, BLK), :]
-                out_ref[owner, pl.ds(slot * BLK, BLK), low : low + HD] = (
+                out_ref[half, owner, pl.ds(row, BLK), low : low + HD] = (
                     piece[:, :HD] * scale
                 ).astype(out_ref.dtype)
-                out_ref[owner, pl.ds(slot * BLK, BLK), low + HD : low + width] = piece[
+                out_ref[half, owner, pl.ds(row, BLK), low + HD : low + width] = piece[
                     :, HD:
                 ].astype(out_ref.dtype)
 
 
 def attention(order, docs, queries, out_grad, lse, dots, kv_all):
-    groups, kv_heads, local_tokens, width = kv_all.shape
+    groups, kv_heads, _, width = kv_all.shape
+    local_tokens = queries.shape[1]
     total = groups * local_tokens
     smem = pl.BlockSpec(memory_space=pltpu.SMEM)
     vmem = pl.BlockSpec(memory_space=pltpu.VMEM)
     return pl.pallas_call(
         attention_kernel,
         out_shape=jax.ShapeDtypeStruct(
-            (groups, local_tokens, kv_heads * width), jnp.bfloat16
+            (2, groups, local_tokens // 2, kv_heads * width), jnp.bfloat16
         ),
         in_specs=[smem, smem] + [vmem] * 5,
         out_specs=vmem,
@@ -142,7 +144,7 @@
     ).astype(out_at.dtype)
 
 
-def line_stage(n, pos, device, source, target, send, recv, sems, looped):
+def line_stage(n, pos, device, source, target, send, recv, sems):
     def copy(side, step, src):
         return pltpu.make_async_remote_copy(
             src_ref=src,
@@ -153,25 +155,25 @@
             device_id_type=MESH,
         )
 
-    def add(out_at, own_at, parts):
-        looped(out_at, own_at, parts)
-
-    for step in range(n - 1):
+    def place_of(side):
+        return pos if side == 0 else n - 1 - pos
+
+    def advance(step):
         for side in (0, 1):
-            place = pos if side == 0 else n - 1 - pos
+            place = place_of(side)
             away = n - 1 - step
             dest = pos + away if side == 0 else pos - away
 
             @pl.when(place == 0)
-            def _(side=side, step=step, dest=dest):
+            def _(side=side, dest=dest):
                 copy(side, step, source(dest)).start()
 
             if step > 0:
 
                 @pl.when((place >= 1) & (place <= step))
-                def _(side=side, step=step, dest=dest):
+                def _(side=side, dest=dest):
                     copy(side, step - 1, send.at[side, step - 1]).wait_recv()
-                    add(send.at[side, step], source(dest), [recv.at[side, step - 1]])
+                    add_rows(send.at[side, step], source(dest), [recv.at[side, step - 1]])
                     copy(side, step, send.at[side, step]).start()
 
     last = n - 2
@@ -179,31 +181,42 @@
     def arrived(side):
         copy(side, last, send.at[side, last]).wait_recv()
 
-    if n > 2:
-
-        @pl.when((pos >= 1) & (pos <= n - 2))
+    def finish():
+        if n > 2:
+
+            @pl.when((pos >= 1) & (pos <= n - 2))
+            def _():
+                arrived(0)
+                arrived(1)
+                add_rows(target, source(pos), [recv.at[0, last], recv.at[1, last]])
+
+        @pl.when(pos == 0)
+        def _():
+            arrived(1)
+            add_rows(target, source(pos), [recv.at[1, last]])
+
+        @pl.when(pos == n - 1)
         def _():
             arrived(0)
-            arrived(1)
-            add(target, source(pos), [recv.at[0, last], recv.at[1, last]])
-
-    @pl.when(pos == 0)
-    def _():
-        arrived(1)
-        add(target, source(pos), [recv.at[1, last]])
-
-    @pl.when(pos == n - 1)
-    def _():
-        arrived(0)
-        add(target, source(pos), [recv.at[0, last]])
-
-    for step in range(n - 1):
-        for side in (0, 1):
-            place = pos if side == 0 else n - 1 - pos
-
-            @pl.when(place <= step)
-            def _(side=side, step=step):
-                copy(side, step, send.at[side, step]).wait_send()
+            add_rows(target, source(pos), [recv.at[0, last]])
+
+    def drain():
+        for step in range(n - 1):
+            for side in (0, 1):
+
+                @pl.when(place_of(side) <= step)
+                def _(side=side, step=step):
+                    copy(side, step, send.at[side, step]).wait_send()
+
+    steps = [functools.partial(advance, step) for step in range(n - 1)] + [finish]
+    return steps, drain
+
+
+def interleave(*lists):
+    for turn in range(max(len(steps) for steps in lists)):
+        for steps in lists:
+            if turn < len(steps):
+                steps[turn]()
 
 
 def add_rows(out_at, own_at, parts):
@@ -239,16 +252,32 @@
     return core_line, chip_line
 
 
-def token_sum_kernel(part_ref, out_ref, half, send_a, recv_a, sem_a, send_b, recv_b, sem_b):
-    chips = part_ref.shape[0]
+def token_sum_kernel(part_ref, out_ref, held, *stages):
+    halves, chips = part_ref.shape[:2]
     core_line, chip_line = context_lines(chips)
     neighbours_barrier([core_line, chip_line])
-    line_stage(
-        *core_line, lambda d: part_ref.at[:, d], half, send_a, recv_a, sem_a, add_rows
-    )
-    line_stage(
-        *chip_line, lambda d: half.at[d], out_ref, send_b, recv_b, sem_b, add_rows
-    )
+    near, far, drains = [], [], []
+    for i in range(halves):
+        work = stages[6 * i : 6 * i + 6]
+        steps, drain = line_stage(
+            *core_line, lambda d, i=i: part_ref.at[i, :, d], held.at[i], *work[:3]
+        )
+        near.append(steps)
+        drains.append(drain)
+        steps, drain = line_stage(
+            *chip_line, lambda d, i=i: held.at[i, d], out_ref.at[i], *work[3:]
+        )
+        far.append(steps)
+        drains.append(drain)
+    for steps in near:
+        for step in steps[:-1]:
+            step()
+    for i in range(halves):
+        near[i][-1]()
+        far[i][0]()
+    interleave(*[steps[1:] for steps in far])
+    for drain in drains:
+        drain()
 
 
 def stage_scratch(n, shape):
@@ -260,16 +289,19 @@
 
 
 def token_sum(parts):
-    chips, cores, slabs, rows, cols = parts.shape
+    halves, chips, cores, slabs, rows, cols = parts.shape
     vmem = pl.BlockSpec(memory_space=pltpu.VMEM)
     return pl.pallas_call(
         token_sum_kernel,
-        out_shape=jax.ShapeDtypeStruct((slabs, rows, cols), jnp.bfloat16),
+        out_shape=jax.ShapeDtypeStruct((halves, slabs, rows, cols), jnp.bfloat16),
         in_specs=[vmem],
         out_specs=vmem,
-        scratch_shapes=[pltpu.VMEM((chips, slabs, rows, cols), jnp.bfloat16)]
-        + stage_scratch(cores, (chips, slabs, rows, cols))
-        + stage_scratch(chips, (slabs, rows, cols)),
+        scratch_shapes=[pltpu.VMEM((halves, chips, slabs, rows, cols), jnp.bfloat16)]
+        + (
+            stage_scratch(cores, (chips, slabs, rows, cols))
+            + stage_scratch(chips, (slabs, rows, cols))
+        )
+        * halves,
         compiler_params=pltpu.CompilerParams(
             collective_id=1, has_side_effects=True, vmem_limit_bytes=VMEM_MAX
         ),
@@ -279,39 +311,55 @@
     )(parts)
 
 
-def final_sum_kernel(
-    part_ref,
-    out_ref,
-    half,
-    quarter,
-    send_a,
-    recv_a,
-    sem_a,
-    send_b,
-    recv_b,
-    sem_b,
-    send_c,
-    recv_c,
-    sem_c,
-):
+def final_sum_kernel(part_ref, out_ref, held, over_dp, over_chips, *stages):
     chips, _, blocks, copies, rows, cols = part_ref.shape
+    some = blocks // 2
     core_line, chip_line = context_lines(chips)
     mine = lax.axis_index("dp")
     dp_line = (copies, mine, lambda d: {"dp": mine + d})
     neighbours_barrier([core_line, dp_line, chip_line])
-    line_stage(
-        *core_line, lambda d: part_ref.at[:, d], half, send_a, recv_a, sem_a, add_rows
-    )
-    line_stage(
-        *dp_line, lambda d: half.at[:, :, d], quarter, send_b, recv_b, sem_b, add_rows
-    )
-    line_stage(
-        *chip_line, lambda d: quarter.at[d], out_ref, send_c, recv_c, sem_c, add_rows
-    )
+    near, drains = [], []
+
+    def stage(index, *args):
+        steps, drain = line_stage(*args, *stages[3 * index : 3 * index + 3])
+        drains.append(drain)
+        return steps
+
+    for i in range(2):
+        near.append(
+            stage(
+                i,
+                *core_line,
+                lambda d, i=i: part_ref.at[:, d, pl.ds(i * some, some)],
+                held.at[i],
+            )
+        )
+    a_dp = stage(2, *dp_line, lambda d: held.at[0, :, :, d], over_dp)
+    a_chip = stage(3, *chip_line, lambda d: over_dp.at[d], out_ref.at[pl.ds(0, some)])
+    b_chip = stage(4, *chip_line, lambda d: held.at[1, d], over_chips)
+    b_dp = stage(
+        5, *dp_line, lambda d: over_chips.at[:, d], out_ref.at[pl.ds(some, some)]
+    )
+    for steps in near:
+        for step in steps[:-1]:
+            step()
+    near[0][-1]()
+    a_dp[0]()
+    near[1][-1]()
+    b_chip[0]()
+    interleave(b_chip[1:-1], a_dp[1:-1])
+    a_dp[-1]()
+    a_chip[0]()
+    b_chip[-1]()
+    b_dp[0]()
+    interleave(a_chip[1:], b_dp[1:])
+    for drain in drains:
+        drain()
 
 
 def final_sum(parts):
     chips, cores, blocks, copies, rows, cols = parts.shape
+    some = blocks // 2
     vmem = pl.BlockSpec(memory_space=pltpu.VMEM)
     return pl.pallas_call(
         final_sum_kernel,
@@ -319,12 +367,15 @@
         in_specs=[vmem],
         out_specs=vmem,
         scratch_shapes=[
-            pltpu.VMEM((chips, blocks, copies, rows, cols), jnp.bfloat16),
-            pltpu.VMEM((chips, blocks, rows, cols), jnp.bfloat16),
+            pltpu.VMEM((2, chips, some, copies, rows, cols), jnp.bfloat16),
+            pltpu.VMEM((chips, some, rows, cols), jnp.bfloat16),
+            pltpu.VMEM((some, copies, rows, cols), jnp.bfloat16),
         ]
-        + stage_scratch(cores, (chips, blocks, copies, rows, cols))
-        + stage_scratch(copies, (chips, blocks, rows, cols))
-        + stage_scratch(chips, (blocks, rows, cols)),
+        + stage_scratch(cores, (chips, some, copies, rows, cols)) * 2
+        + stage_scratch(copies, (chips, some, rows, cols))
+        + stage_scratch(chips, (some, rows, cols))
+        + stage_scratch(chips, (some, copies, rows, cols))
+        + stage_scratch(copies, (some, rows, cols)),
         compiler_params=pltpu.CompilerParams(
             collective_id=2, has_side_effects=True, vmem_limit_bytes=VMEM_MAX
         ),
@@ -355,12 +406,18 @@
     chips = groups // 2
     slots = local_tokens // BLK
 
-    kv_own = jnp.concatenate([key_states[0], value_states[0]], axis=-1)
-    kv_all = lax.all_gather(kv_own, "context", axis=0, tiled=False)
-
+    own_blocks = sign_vector.shape[0]
     factor = 1.0 / jnp.left_shift(jnp.int32(1), exponents[0]).astype(jnp.float32)
     signs = (sign_vector.astype(jnp.float32) * factor[:, None]).astype(jnp.bfloat16)
-    signs_all = lax.all_gather(signs, "context", axis=0, tiled=True)
+    tail = jnp.pad(signs, ((0, 16 - own_blocks), (0, HD)))
+    kv_own = jnp.concatenate([key_states[0], value_states[0]], axis=-1)
+    kv_own = jnp.concatenate(
+        [kv_own, jnp.broadcast_to(tail[None], (local_kv, 16, 2 * HD))], axis=1
+    )
+    kv_all = lax.all_gather(kv_own, "context", axis=0, tiled=False)
+    signs_all = kv_all[:, 0, local_tokens : local_tokens + own_blocks, :HD].reshape(
+        groups * own_blocks, HD
+    )
     local_blocks = layer_input.shape[2] // HB
     signs_own = lax.dynamic_slice_in_dim(
         signs_all, lax.axis_index("tensor") * local_blocks, local_blocks, 0
@@ -392,14 +449,13 @@
         row_stats(grad_dots),
         kv_all,
     )
-    slabs = 4
+    slabs = 2
     kv_grad = token_sum(
-        parts.reshape(chips, 2, slabs, local_tokens // slabs, local_cols)
+        parts.reshape(2, chips, 2, slabs, local_tokens // slabs // 2, local_cols)
     ).reshape(local_tokens, local_cols)
     member = jnp.dot(rotated_all, kv_grad, preferred_element_type=jnp.float32).astype(
         jnp.bfloat16
     )
-    own_blocks = sign_vector.shape[0]
     return final_sum(
         member.reshape(chips, 2, own_blocks, copies, HB // copies, local_cols)
     )

time: 197 us -> 185 us (0.939)
  Pallas kernels: 122 us -> 102 us
  waiting for transfers between devices: 30 us -> 49 us
  blocking collectives: 13.5 us -> 0 us
    all_gather x1, waiting for transfers between devices: 30 us -> 49 us  [per_device(): kv_all = lax.all_gather(kv_own, 'context', axis=0, tiled=False)]
    all_gather x1 -> x0, blocking collectives: 13.5 us -> none  [per_device(): signs_all = lax.all_gather(signs, 'context', axis=0, tiled=True)]
    pallas_call x1, Pallas kernels: 53.6 us -> 42.6 us  [final_sum(): pl.pallas_call(final_sum_kernel, out_shape=jax.ShapeDtypeStruct((blocks,...]
    pallas_call x2, Pallas kernels: 68.2 us -> 59.6 us  [the longest x1 40.7 us: token_sum(): pl.pallas_call(token_sum_kernel, out_shape=jax.ShapeDtypeStruct((halves,...]
    unnamed x10 -> x6, local copies, waits for them, and re-layouts: 4.09 us -> 4.74 us
  transfers between devices with their start and end apart: 2 -> 2, of which waited for: 1 -> 1; matrix products, arithmetic and copies ran while one was open for 3% -> 2% of each run, Pallas kernels for 35% -> 32%
where the time goes in v2:
time: 185 us
  Pallas kernels  102 us (55%)
  waiting for transfers between devices  49 us (26%)
  between operations  13.5 us (7%)
  matrix products  9.46 us (5%)
  local copies, waits for them, and re-layouts  7.12 us (4%)
  other arithmetic  3.38 us (2%)
    all_gather x1, waiting for transfers between devices, per_device(): kv_all = lax.all_gather(kv_own, 'context', axis=0, tiled=False)  49 us
    pallas_call x1, Pallas kernels, final_sum(): pl.pallas_call(final_sum_kernel, out_shape=jax.ShapeDtypeStruct((blocks,...  42.6 us
    pallas_call x1, Pallas kernels, token_sum(): pl.pallas_call(token_sum_kernel, out_shape=jax.ShapeDtypeStruct((halves,...  40.7 us
    pallas_call x1, Pallas kernels, attention(): pl.pallas_call(attention_kernel, out_shape=jax.ShapeDtypeStruct((2, group...  18.9 us
    dot_general x1, matrix products, per_device(): jnp.dot(rotated_all, kv_grad, preferred_element_type=jnp.float32)  6.72 us
    unnamed x6, local copies, waits for them, and re-layouts  4.74 us
  transfers between devices with their start and end apart: 2, of which 1 were waited for; matrix products, arithmetic and copies ran while one was open for 2% of the time, Pallas kernels for 32%

profile of v2, /device:TPU:0, one launch (start us, length us, event | category | flops | bytes accessed | tf_op | source)
XLA Modules:
  0.0 184.6 jit_solution(11009972412372096660)
XLA Ops:
  6.5 0.0 all-gather.6.cloned.1.call-start
  6.5 0.7 divide_bitcast_fusion
  7.2 0.8 multiply_convert_fusion.3
  8.0 1.9 %pad_maximum_fusion = bf16[2,528,256]{2,1,0:T(8,128)(2,1)} fusion(bf16[2,16,256]{2,1,0:T(8,128)(2,1)S(1)} %broadcast_in_dim.2, bf16[2,512,128]{2,1,0:T(8,128)(2,1)} %bitcast.31, bf16[2,512,128]{2,1,0:T(8,128)(2,1)} %bitcast.32), kind=kLoop, calls=%fused_computation.4 | loop fusion | flops 1622016 | bytes 1081344 | tf_op jit(solution)/shard_map/concatenate | solution.py:414
  9.9 0.0 all-gather.6.cloned.1.call-update
  9.9 0.0 all-gather.4.cloned.1.call-start
  9.9 2.2 %copy.18 = bf16[64,8,16,128]{3,2,1,0:T(8,128)(2,1)S(1)} copy(bf16[64,8,16,128]{3,1,2,0:T(8,128)(2,1)} %bitcast.27) | data formatting | bytes 4194304
  12.1 0.1 subtract_convert_fusion
  12.2 49.0 %all-gather.6.cloned.1.call-done = bf16[16,528,256]{2,1,0:T(8,128)(2,1)} async-done(((bf16[2,528,256]{2,1,0:T(8,128)(2,1)}), bf16[16,528,256]{2,1,0:T(8,128)(2,1)}) %all-gather.6.cloned.1.call-update) | async-done | bytes 4325392 | tf_op jit(solution)/shard_map/all_gather | solution.py:417
  61.2 0.7 slice.4
  61.9 2.7 %multiply_convert_fusion = bf16[16,128,512]{2,1,0:T(8,128)(2,1)} fusion(bf16[512,16,128]{2,1,0:T(8,128)(2,1)S(1)} %bitcast.24, f32[16,128]{1,0:T(8,128)S(1)} %dynamic-slice_convert_fusion, f32[128,128]{1,0:T(8,128)S(1)} %subtract_convert_fusion), kind=kOutput, calls=%fused_computation.1 | convolution fusion | flops 271056896 | bytes 4268032 | tf_op jit(solution)/shard_map/bij,tbj->bit/dot_general | solution.py:427
  64.7 0.0 copy-start
  64.7 0.0 copy-start.1
  64.7 0.0 all-gather.4.cloned.1.call-update
  64.7 0.7 copy-done
  65.4 0.1 reshape.95
  65.5 0.7 reshape.89.lse_ref
  66.2 0.0 copy-done.1
  66.2 0.1 reshape.97
  66.3 0.7 reshape.91.dots_ref
  67.0 18.9 %shard_map.109 = bf16[2,8,256,512]{3,2,1,0:T(8,128)(2,1)} custom-call(s32[1,128]{1,0:T(1,128)} %order_ref.1, s32[1,10]{1,0:T(1,128)} %docs_ref.1, bf16[8,512,128]{2,1,0:T(8,128)(2,1)} %bitcast.36, bf16[8,512,128]{2,1,0:T(8,128)(2,1)} %bitcast.37, f32[16,2,128]{2,1,0:T(2,128)} %reshape.89.lse_ref, f32[16,2,128]{2,1,0:T(2,128)} %reshape.91.dots_ref, ...), custom_call_target="tpu_custom_call" | custom-call | flops 4000000000 | bytes 14680064 | tf_op jit(solution)/shard_map/pallas_call | solution.py:123
  86.0 40.7 %shard_map.110 = bf16[2,2,128,512]{3,2,1,0:T(8,128)(2,1)} custom-call(bf16[2,4,2,2,128,512]{5,4,3,2,1,0:T(8,128)(2,1)} %bitcast.25), custom_call_target="tpu_custom_call" | custom-call | flops 10000000 | bytes 5242880 | tf_op jit(solution)/shard_map/pallas_call | solution.py:294
  126.6 0.0 all-gather.4.cloned.1.call-done
  126.6 6.7 %convolution_convert_fusion = bf16[4096,512]{1,0:T(8,128)(2,1)} fusion(bf16[4096,512]{1,0:T(8,128)(2,1)} %all-gather.4.cloned.1.call-done, bf16[512,512]{1,0:T(8,128)(2,1)} %bitcast.28), kind=kOutput, calls=%fused_computation | convolution fusion | flops 2149580800 | bytes 8912896 | tf_op jit(solution)/shard_map/dot_general | solution.py:456
  133.4 42.6 %shard_map.111 = f32[4,64,512]{2,1,0:T(8,128)} custom-call(bf16[4,2,4,2,64,512]{5,4,3,2,1,0:T(8,128)(2,1)} %bitcast.26), custom_call_target="tpu_custom_call" | custom-call | flops 10000000 | bytes 5242880 | tf_op jit(solution)/shard_map/pallas_call | solution.py:364
  175.9 1.9 %copy.26 = f32[4,64,512]{2,1,0:T(8,128)} copy(f32[4,64,512]{2,1,0:T(8,128)} %shard_map.111) | data formatting | bytes 1048576
  (5 shorter events, 0.1 us)
Async XLA Ops:
  6.5 54.7 %all-gather.6.cloned.1.call-start = ((), (), s32[]{:S(2)}) async-start(), calls=%async_computation.1 | async-start | bytes 4866048 | tf_op jit(solution)/shard_map/all_gather | solution.py:417
  9.9 116.8 %all-gather.4.cloned.1.call-start = ((), (), s32[]{:S(2)}) async-start(), calls=%async_computation | async-start | bytes 6291456 | tf_op jit(solution)/shard_map/all_gather | solution.py:435
  64.7 0.7 copy-start
  64.7 1.5 copy-start.1
Sparse Core Ops, SparseCore 0:
  10.0 51.1 all-gather.5
  64.8 55.4 all-gather.3

commit v3 on v2

--- a/solution.py
+++ b/solution.py
@@ -104,7 +104,7 @@
             place = pl.multiple_of(PAD + order_ref[0, owner * slots + slot] * BLK, BLK)
             for head in range(kv_heads):
                 low = head * width
-                half, row = divmod(slot * BLK, local_tokens // 2)
+                half, row = divmod(slot * BLK, local_tokens // 4)
                 piece = acc[head, pl.ds(place, BLK), :]
                 out_ref[half, owner, pl.ds(row, BLK), low : low + HD] = (
                     piece[:, :HD] * scale
@@ -123,7 +123,7 @@
     return pl.pallas_call(
         attention_kernel,
         out_shape=jax.ShapeDtypeStruct(
-            (2, groups, local_tokens // 2, kv_heads * width), jnp.bfloat16
+            (4, groups, local_tokens // 4, kv_heads * width), jnp.bfloat16
         ),
         in_specs=[smem, smem] + [vmem] * 5,
         out_specs=vmem,
@@ -451,7 +451,7 @@
     )
     slabs = 2
     kv_grad = token_sum(
-        parts.reshape(2, chips, 2, slabs, local_tokens // slabs // 2, local_cols)
+        parts.reshape(4, chips, 2, slabs, local_tokens // slabs // 4, local_cols)
     ).reshape(local_tokens, local_cols)
     member = jnp.dot(rotated_all, kv_grad, preferred_element_type=jnp.float32).astype(
         jnp.bfloat16

time: 185 us -> 184 us (level)
    pallas_call x1, Pallas kernels: 40.7 us -> 42.5 us  [token_sum(): pl.pallas_call(token_sum_kernel, out_shape=jax.ShapeDtypeStruct((halves,...]
  transfers between devices with their start and end apart: 2 -> 2, of which waited for: 1 -> 1; matrix products, arithmetic and copies ran while one was open for 2% -> 2% of each run, Pallas kernels for 32% -> 33%
where the time goes in v3:
time: 184 us
  Pallas kernels  102 us (55%)
  waiting for transfers between devices  49 us (27%)
  between operations  13.5 us (7%)
  matrix products  9.46 us (5%)
  local copies, waits for them, and re-layouts  7.12 us (4%)
  other arithmetic  3.38 us (2%)
    all_gather x1, waiting for transfers between devices, per_device(): kv_all = lax.all_gather(kv_own, 'context', axis=0, tiled=False)  49 us
    pallas_call x1, Pallas kernels, token_sum(): pl.pallas_call(token_sum_kernel, out_shape=jax.ShapeDtypeStruct((halves,...  42.5 us
    pallas_call x1, Pallas kernels, final_sum(): pl.pallas_call(final_sum_kernel, out_shape=jax.ShapeDtypeStruct((blocks,...  41.1 us
    pallas_call x1, Pallas kernels, attention(): pl.pallas_call(attention_kernel, out_shape=jax.ShapeDtypeStruct((4, group...  17.9 us
    dot_general x1, matrix products, per_device(): jnp.dot(rotated_all, kv_grad, preferred_element_type=jnp.float32)  6.72 us
    unnamed x6, local copies, waits for them, and re-layouts  4.74 us
  transfers between devices with their start and end apart: 2, of which 1 were waited for; matrix products, arithmetic and copies ran while one was open for 2% of the time, Pallas kernels for 33%

profile of v3, /device:TPU:0, one launch (start us, length us, event | category | flops | bytes accessed | tf_op | source)
XLA Modules:
  0.0 184.0 jit_solution(11608744276068307024)
XLA Ops:
  6.5 0.0 all-gather.6.cloned.1.call-start
  6.5 0.7 divide_bitcast_fusion
  7.2 0.8 multiply_convert_fusion.3
  8.0 1.9 %pad_maximum_fusion = bf16[2,528,256]{2,1,0:T(8,128)(2,1)} fusion(bf16[2,16,256]{2,1,0:T(8,128)(2,1)S(1)} %broadcast_in_dim.2, bf16[2,512,128]{2,1,0:T(8,128)(2,1)} %bitcast.31, bf16[2,512,128]{2,1,0:T(8,128)(2,1)} %bitcast.32), kind=kLoop, calls=%fused_computation.4 | loop fusion | flops 1622016 | bytes 1081344 | tf_op jit(solution)/shard_map/concatenate | solution.py:414
  9.9 0.0 all-gather.6.cloned.1.call-update
  9.9 0.0 all-gather.4.cloned.1.call-start
  9.9 2.2 %copy.18 = bf16[64,8,16,128]{3,2,1,0:T(8,128)(2,1)S(1)} copy(bf16[64,8,16,128]{3,1,2,0:T(8,128)(2,1)} %bitcast.27) | data formatting | bytes 4194304
  12.1 0.1 subtract_convert_fusion
  12.2 49.0 %all-gather.6.cloned.1.call-done = bf16[16,528,256]{2,1,0:T(8,128)(2,1)} async-done(((bf16[2,528,256]{2,1,0:T(8,128)(2,1)}), bf16[16,528,256]{2,1,0:T(8,128)(2,1)}) %all-gather.6.cloned.1.call-update) | async-done | bytes 4325392 | tf_op jit(solution)/shard_map/all_gather | solution.py:417
  61.2 0.7 slice.4
  61.9 2.7 %multiply_convert_fusion = bf16[16,128,512]{2,1,0:T(8,128)(2,1)} fusion(bf16[512,16,128]{2,1,0:T(8,128)(2,1)S(1)} %bitcast.24, f32[16,128]{1,0:T(8,128)S(1)} %dynamic-slice_convert_fusion, f32[128,128]{1,0:T(8,128)S(1)} %subtract_convert_fusion), kind=kOutput, calls=%fused_computation.1 | convolution fusion | flops 271056896 | bytes 4268032 | tf_op jit(solution)/shard_map/bij,tbj->bit/dot_general | solution.py:427
  64.7 0.0 copy-start
  64.7 0.0 copy-start.1
  64.7 0.0 all-gather.4.cloned.1.call-update
  64.7 0.7 copy-done
  65.4 0.1 reshape.95
  65.5 0.7 reshape.89.lse_ref
  66.2 0.0 copy-done.1
  66.2 0.1 reshape.97
  66.3 0.7 reshape.91.dots_ref
  67.0 17.9 %shard_map.109 = bf16[4,8,128,512]{3,2,1,0:T(8,128)(2,1)} custom-call(s32[1,128]{1,0:T(1,128)} %order_ref.1, s32[1,10]{1,0:T(1,128)} %docs_ref.1, bf16[8,512,128]{2,1,0:T(8,128)(2,1)} %bitcast.36, bf16[8,512,128]{2,1,0:T(8,128)(2,1)} %bitcast.37, f32[16,2,128]{2,1,0:T(2,128)} %reshape.89.lse_ref, f32[16,2,128]{2,1,0:T(2,128)} %reshape.91.dots_ref, ...), custom_call_target="tpu_custom_call" | custom-call | flops 4000000000 | bytes 14680064 | tf_op jit(solution)/shard_map/pallas_call | solution.py:123
  84.9 42.5 %shard_map.110 = bf16[4,2,64,512]{3,2,1,0:T(8,128)(2,1)} custom-call(bf16[4,4,2,2,64,512]{5,4,3,2,1,0:T(8,128)(2,1)} %bitcast.25), custom_call_target="tpu_custom_call" | custom-call | flops 10000000 | bytes 5242880 | tf_op jit(solution)/shard_map/pallas_call | solution.py:294
  127.5 0.0 all-gather.4.cloned.1.call-done
  127.5 6.7 %convolution_convert_fusion = bf16[4096,512]{1,0:T(8,128)(2,1)} fusion(bf16[4096,512]{1,0:T(8,128)(2,1)} %all-gather.4.cloned.1.call-done, bf16[512,512]{1,0:T(8,128)(2,1)} %bitcast.28), kind=kOutput, calls=%fused_computation | convolution fusion | flops 2149580800 | bytes 8912896 | tf_op jit(solution)/shard_map/dot_general | solution.py:456
  134.2 41.1 %shard_map.111 = f32[4,64,512]{2,1,0:T(8,128)} custom-call(bf16[4,2,4,2,64,512]{5,4,3,2,1,0:T(8,128)(2,1)} %bitcast.26), custom_call_target="tpu_custom_call" | custom-call | flops 10000000 | bytes 5242880 | tf_op jit(solution)/shard_map/pallas_call | solution.py:364
  175.3 1.9 %copy.26 = f32[4,64,512]{2,1,0:T(8,128)} copy(f32[4,64,512]{2,1,0:T(8,128)} %shard_map.111) | data formatting | bytes 1048576
  (5 shorter events, 0.1 us)
Async XLA Ops:
  6.5 54.7 %all-gather.6.cloned.1.call-start = ((), (), s32[]{:S(2)}) async-start(), calls=%async_computation.1 | async-start | bytes 4866048 | tf_op jit(solution)/shard_map/all_gather | solution.py:417
  9.9 117.6 %all-gather.4.cloned.1.call-start = ((), (), s32[]{:S(2)}) async-start(), calls=%async_computation | async-start | bytes 6291456 | tf_op jit(solution)/shard_map/all_gather | solution.py:435
  64.7 0.7 copy-start
  64.7 1.5 copy-start.1
Sparse Core Ops, SparseCore 0:
  10.0 51.1 all-gather.5
  64.8 55.4 all-gather.3
